TPU v7x, 32 devices: a whole 2x2x4 slice. The times are simulated.
32 devices in a mesh: groups: 2 (over y), space: 4 (over z), comp: 2 (over x), sub: 2 (over core).
Axes of the slice: x: 2, y: 2, z: 4, core: 2. Of those that a mesh axis runs over, the one named last changes fastest.
Arguments:
- spectrum: float32 [32, 512, 864], P(('groups', 'sub'), ('space', 'comp')), parts along dimension 0, may hold values from 0.05 to 1
- wind_speed: float32 [32, 512], P(('groups', 'sub'), ('space', 'comp')), parts along dimension 0, may hold values from 2 to 10
- wind_dir: float32 [32, 512], P(('groups', 'sub'), ('space', 'comp')), parts along dimension 0, may hold values from -3.140625 to 3.140625
- ocean_mask: int32 [16, 512], P('sub', 'space'), may hold values 0 or 1
- turning: float32 [16, 512], P('sub', 'space'), may hold values from -0.8 to 0.8
- u_current: float32 [16], P('sub'), may hold values from -0.35 to 0.35
- group_courant: float32 [24], replicated, may hold values from 0.2 to 0.55
- growth_rate: float32 [24], replicated, may hold values from 0.02 to 0.08
- dissipation: float32 [24], replicated, may hold values from 0.2 to 0.6
- comp_owner: int32 [24], replicated, may hold values from 0 to 23, each once
Outputs:
- propagated: float32 [24, 36, 32, 512], P('comp', None, ('groups', 'sub'), 'space'), parts along dimension 2
There are 2 independent parts, one for each index of `groups`. A program takes and returns all parts, laid end to end along the dimension named above; an argument that names none is the same for every part. Nothing has to cross between parts.
Inputs may be any that keep to these rules, and one draw needn't show every extreme that they name: `comp_owner`: each of the 24 frequencies appears once.
All inputs are finite; a program needn't handle non-finite values. No bound on the sum of `ocean_mask` on one device may be relied on, other than what follows from the above.
Results may differ from a plain program's by a relative error of at most 0.0003.
Values sent between devices are 32-bit elements; how exact they have to be, the bound alone decides.
A program may use at most 128 MiB of HBM per device.

v0:
```python
import functools
import math

import jax
import jax.numpy as jnp
import numpy as np
from jax import lax
from jax.experimental import pallas as pl
from jax.experimental.pallas import tpu as pltpu
from jax.sharding import PartitionSpec as P

NSUB = 4
HALO = 2 * NSUB
PER_PACK = 12
ROWS = 8
LANES = 128


def weights(courant):
    s = jnp.abs(courant)
    q = (1.0 - s * s) / 6.0
    sq = s * q
    up2 = -sq
    up1 = s * (0.5 + 0.5 * s) + 3.0 * sq
    mid = 1.0 - s * s - 3.0 * sq
    down = sq - s * (0.5 - 0.5 * s)
    return up2, up1, mid, down


def kernel(
    sizes,
    xt,
    wind_speed,
    wind_dir,
    mask,
    turning,
    current,
    speed,
    growth,
    loss,
    owner,
    cosines,
    sines,
    out,
    tables,
    level_part,
    sendbuf,
    recv,
    main,
    small,
    small_sib,
    small_left,
    small_right,
    mask_all,
    turn_all,
    halo_out,
    halo_in,
    spin,
    res,
    send_sem,
    recv_sem,
    small_send,
    small_recv,
    halo_send,
    halo_recv,
    out_send,
    out_recv,
    own_sem,
):
    ncomp, nspace, ndirs, nfreqs, per_core = sizes
    strip = LANES // ncomp
    nd = ndirs // ncomp
    half = ndirs // 2
    packs = ndirs // PER_PACK
    me_c = lax.axis_index("comp")
    me_s = lax.axis_index("sub")
    me_z = lax.axis_index("space")
    other = 1 - me_s
    right = lax.rem(me_z + 1, nspace)
    left = lax.rem(me_z + nspace - 1, nspace)
    MESH = pl.DeviceIdType.MESH
    lane = lax.broadcasted_iota(jnp.int32, (ROWS, LANES), 1)
    row = lax.broadcasted_iota(jnp.int32, (ROWS, LANES), 0)

    def peer(co, so):
        return {"comp": lax.rem(me_c + co, ncomp), "sub": lax.rem(me_s + so, 2)}

    peers = [(co, so) for co in range(ncomp) for so in range(2) if co or so]
    near = [{"space": z, "sub": s} for z in (left, right) for s in (me_s, other)]
    barrier = pltpu.get_barrier_semaphore()
    for co, so in peers:
        pl.semaphore_signal(barrier, inc=1, device_id=peer(co, so), device_id_type=MESH)
    for to in near:
        pl.semaphore_signal(barrier, inc=1, device_id=to, device_id_type=MESH)

    level_part[...] = jnp.zeros_like(level_part)

    def add_level(f, carry):
        for part in range(4):
            block = xt[pl.ds(f * ndirs + part * (ndirs // 4), ndirs // 4)]
            level_part[part] += jnp.sum(block, axis=0)
        return carry

    lax.fori_loop(0, nfreqs, add_level, 0)
    level = (level_part[0] + level_part[1] + level_part[2] + level_part[3]) / (nfreqs * ndirs)
    level = level / (level + 0.25)

    def tiled(a):
        return jnp.concatenate([a] * ncomp, axis=1)

    level = tiled(level)
    wind = tiled(wind_speed[...])
    toward = tiled(wind_dir[...])
    group = (lane // strip) * nd
    for dd in range(nd):
        angle = 2.0 * math.pi * (group + dd).astype(jnp.float32) / ndirs
        tables[dd] = wind * jnp.maximum(jnp.cos(angle - toward), 0.0)

    small[0] = mask[...]
    small[1] = turning[...]
    small[2] = current[...]
    pl.semaphore_wait(barrier, len(peers) + len(near))

    def fill(dst, at, co, so, kk):
        dest = peer(co, so)
        k = (dest["comp"] * 2 + dest["sub"]) * per_core + kk
        f = owner[k]
        g_rate = growth[f]
        d_rate = loss[f]
        for dd in range(nd):
            parts = [xt[f * ndirs + g * nd + dd] for g in range(ncomp)]
            tile = jnp.concatenate(parts, axis=1)
            dst[at, kk, dd] = tile * jnp.exp(g_rate * tables[dd] - d_rate * level)

    def block_copy(co, so, kk):
        r = co * 2 + so
        return pltpu.make_async_remote_copy(
            src_ref=sendbuf.at[r, kk],
            dst_ref=recv.at[r, kk],
            send_sem=send_sem.at[r, kk],
            recv_sem=recv_sem.at[r, kk],
            device_id=peer(co, so),
            device_id_type=MESH,
        )

    def send_far(kk, carry):
        for co, so in peers:
            if co:
                fill(sendbuf, co * 2 + so, co, so, kk)
                block_copy(co, so, kk).start()
        return carry

    lax.fori_loop(0, per_core, send_far, 0)

    def small_copies():
        sib = pltpu.make_async_remote_copy(
            src_ref=small, dst_ref=small_sib, send_sem=small_send.at[0], recv_sem=small_recv.at[0],
            device_id={"sub": other}, device_id_type=MESH)
        copies = [sib]
        for n, (z, land) in enumerate(((right, small_left), (left, small_right))):
            for so in range(2):
                i = 1 + 2 * n + so
                copies.append(pltpu.make_async_remote_copy(
                    src_ref=small.at[0], dst_ref=land.at[so], send_sem=small_send.at[i],
                    recv_sem=small_recv.at[i],
                    device_id={"space": z, "sub": lax.rem(me_s + so, 2)}, device_id_type=MESH))
        return copies

    for copy in small_copies():
        copy.start()

    def send_near(kk, carry):
        fill(sendbuf, 1, 0, 1, kk)
        block_copy(0, 1, kk).start()
        fill(recv, 0, 0, 0, kk)
        return carry

    lax.fori_loop(0, per_core, send_near, 0)

    for copy in small_copies():
        copy.wait()

    first = me_s == 0

    def both(own, sib):
        return jnp.where(first, own, sib), jnp.where(first, sib, own)

    def windows(lo, hi, lo_left, hi_left, lo_right, hi_right):
        acc = jnp.zeros((ROWS, LANES), jnp.float32)
        for base, own, l_halo, r_halo in ((0, lo, lo_left, lo_right), (64, hi, hi_left, hi_right)):
            for tile, start, count, at in (
                (own, LANES - 16, 16, 0),
                (r_halo, 0, HALO, 16),
                (l_halo, LANES - HALO, HALO, 24),
                (own, 0, 16, 32),
            ):
                moved = pltpu.roll(tile, (base + at - start) % LANES, 1)
                here = (lane >= base + at) & (lane < base + at + count)
                acc = jnp.where(here, moved, acc)
        return acc

    lo, hi = both(small[0], small_sib[0])
    lo_left, hi_left = both(small_left[0], small_left[1])
    lo_right, hi_right = both(small_right[0], small_right[1])
    mask_all[0] = lo
    mask_all[1] = hi
    mask_all[2] = windows(lo, hi, lo_left, hi_left, lo_right, hi_right)
    lo, hi = both(small[1], small_sib[1])
    for h, c in ((0, lo), (1, hi)):
        for i, w in enumerate(weights(c)):
            turn_all[h, i] = w
        turn_all[h, 4] = c
    lo, hi = both(small[2], small_sib[2])
    mask_all[3] = lo
    mask_all[4] = hi
    mask_all[5] = jnp.where(lane < 64, lo, hi)

    def halo_copy(side, kk):
        to = left if side == 0 else right
        return pltpu.make_async_remote_copy(
            src_ref=halo_out.at[side, kk],
            dst_ref=halo_in.at[side, kk],
            send_sem=halo_send.at[side, kk],
            recv_sem=halo_recv.at[side, kk],
            device_id={"space": to},
            device_id_type=MESH,
        )

    def assemble(kk):
        for co, so in peers:
            block_copy(co, so, kk).wait_recv()
        for h in range(2):
            so = lax.rem(h + me_s, 2)
            sea = mask_all[h]
            for dd in range(nd):
                got = [recv[lax.rem(me_c + ncomp - c, ncomp) * 2 + so, kk, dd] for c in range(ncomp)]
                for g in range(ncomp):
                    tile = got[0] if g == 0 else pltpu.roll(got[0], (LANES - g * strip) % LANES, 1)
                    for c in range(1, ncomp):
                        part = got[c]
                        if c != g:
                            part = pltpu.roll(part, ((c - g) * strip) % LANES, 1)
                        tile = jnp.where(lane < c * strip, tile, part)
                    main[kk, h, g * nd + dd] = tile * sea
            for q in range(packs):
                lows = jnp.zeros((ROWS, LANES), jnp.float32)
                highs = lows
                for j in range(PER_PACK):
                    tile = main[kk, h, q * PER_PACK + j]
                    at = j * HALO
                    here = (lane >= at) & (lane < at + HALO)
                    low = tile if at == 0 else pltpu.roll(tile, at, 1)
                    lows = jnp.where(here, low, lows)
                    highs = jnp.where(here, pltpu.roll(tile, at + HALO, 1), highs)
                halo_out[0, kk, h * packs + q] = lows
                halo_out[1, kk, h * packs + q] = highs
        halo_copy(0, kk).start()
        halo_copy(1, kk).start()

    def along_lon(f, w, up, sea):
        up2, before, mid, after = w
        for _ in range(NSUB):
            far = jnp.where(up, pltpu.roll(f, 2, 1), pltpu.roll(f, LANES - 2, 1))
            near_sum = before * pltpu.roll(f, 1, 1) + after * pltpu.roll(f, LANES - 1, 1)
            f = (mid * f + up2 * far + near_sum) * sea
        return f

    def along_lat(lo, hi, c, forward, sea_lo, sea_hi):
        up2, up1, mid, down = weights(c)
        for _ in range(NSUB):
            if forward:
                a, b = lo, hi

                def shift(n):
                    ra, rb = pltpu.roll(a, n, 0), pltpu.roll(b, n, 0)
                    return jnp.where(row < n, 0.0, ra), jnp.where(row < n, ra, rb)

                rb1, ra1 = pltpu.roll(hi, ROWS - 1, 0), pltpu.roll(lo, ROWS - 1, 0)
                lo_dn = jnp.where(row < ROWS - 1, ra1, rb1)
                hi_dn = jnp.where(row < ROWS - 1, rb1, 0.0)
            else:
                a, b = lo, hi

                def shift(n):
                    ra, rb = pltpu.roll(a, ROWS - n, 0), pltpu.roll(b, ROWS - n, 0)
                    return jnp.where(row < ROWS - n, ra, rb), jnp.where(row < ROWS - n, rb, 0.0)

                ra1, rb1 = pltpu.roll(lo, 1, 0), pltpu.roll(hi, 1, 0)
                lo_dn = jnp.where(row < 1, 0.0, ra1)
                hi_dn = jnp.where(row < 1, ra1, rb1)
            lo1, hi1 = shift(1)
            lo2, hi2 = shift(2)
            lo = (mid * lo + up1 * lo1 + (up2 * lo2 + down * lo_dn)) * sea_lo
            hi = (mid * hi + up1 * hi1 + (up2 * hi2 + down * hi_dn)) * sea_hi
        return lo, hi

    def propagate(kk):
        halo_copy(0, kk).wait_recv()
        halo_copy(1, kk).wait_recv()
        k = (me_c * 2 + me_s) * per_core + kk
        pace = speed[owner[k]]

        def one(q, j, d, forward):
            lo, hi = main[kk, 0, d], main[kk, 1, d]
            edge = jnp.zeros((ROWS, LANES), jnp.float32)
            for h, tile in ((0, lo), (1, hi)):
                base = 64 * h
                before = halo_in[1, kk, h * packs + q]
                after = halo_in[0, kk, h * packs + q]
                for source, start, count, at in (
                    (tile, LANES - 16, 16, 0),
                    (after, j * HALO, HALO, 16),
                    (before, j * HALO, HALO, 24),
                    (tile, 0, 16, 32),
                ):
                    amount = (base + at - start) % LANES
                    moved = source if amount == 0 else pltpu.roll(source, amount, 1)
                    here = (lane >= base + at) & (lane < base + at + count)
                    edge = jnp.where(here, moved, edge)
            c0 = pace * cosines[d]
            done = []
            for i, tile in enumerate((lo, hi, edge)):
                c = c0 + mask_all[3 + i]
                up2, up1, mid, down = weights(c)
                up = c > 0
                w = (up2, jnp.where(up, up1, down), mid, jnp.where(up, down, up1))
                done.append(along_lon(tile, w, up, mask_all[i]))
            lo, hi, edge = done
            fixed = []
            for h, tile in ((0, lo), (1, hi)):
                base = 64 * h
                tile = jnp.where(lane < HALO, pltpu.roll(edge, (LANES - base - 32) % LANES, 1), tile)
                tile = jnp.where(
                    lane >= LANES - HALO, pltpu.roll(edge, (LANES - 16 - base) % LANES, 1), tile)
                fixed.append(tile)
            lo, hi = along_lat(fixed[0], fixed[1], pace * sines[d], forward, mask_all[0], mask_all[1])
            spin[0, 0, d] = lo
            spin[0, 1, d] = hi

        for d in range(ndirs):
            one(d // PER_PACK, d % PER_PACK, d, d < half)

        def turn(h, carry):
            up2, up1, mid, down = (turn_all[h, i] for i in range(4))
            up = turn_all[h, 4] > 0
            before, after = jnp.where(up, up1, down), jnp.where(up, down, up1)
            for step in range(NSUB):
                for d in range(ndirs):
                    f = [spin[step % 2, h, (d + n) % ndirs] for n in (-2, -1, 0, 1, 2)]
                    new = (mid * f[2] + up2 * jnp.where(up, f[0], f[4])) + (before * f[1] + after * f[3])
                    if step == NSUB - 1:
                        res[kk, h, d] = new
                    else:
                        spin[(step + 1) % 2, h, d] = new
            return carry

        lax.fori_loop(0, 2, turn, 0)
        for copy in out_copies(kk):
            copy.start()

    def out_copies(kk):
        slot = me_s * per_core + kk
        own = pltpu.make_async_copy(res.at[kk, me_s], out.at[slot], own_sem.at[kk])
        far = pltpu.make_async_remote_copy(
            src_ref=res.at[kk, other], dst_ref=out.at[slot], send_sem=out_send.at[kk],
            recv_sem=out_recv.at[kk], device_id={"sub": other}, device_id_type=MESH)
        return own, far

    def run(kk, carry):
        @pl.when(kk < per_core)
        def _():
            assemble(kk)

        @pl.when(kk > 0)
        def _():
            propagate(kk - 1)

        return carry

    lax.fori_loop(0, per_core + 1, run, 0)

    def drain(kk, carry):
        for copy in out_copies(kk):
            copy.wait()
        for co, so in peers:
            block_copy(co, so, kk).wait_send()
        halo_copy(0, kk).wait_send()
        halo_copy(1, kk).wait_send()
        return carry

    lax.fori_loop(0, per_core, drain, 0)


def per_device(
    ncomp,
    nspace,
    spectrum,
    wind_speed,
    wind_dir,
    ocean_mask,
    turning,
    u_current,
    group_courant,
    growth_rate,
    dissipation,
    comp_owner,
):
    rows, strip, ncomps = spectrum.shape
    nfreqs = group_courant.shape[0]
    ndirs = ncomps // nfreqs
    nd = ndirs // ncomp
    owned = nfreqs // ncomp
    per_core = owned // 2
    npeer = ncomp * 2
    packs = ndirs // PER_PACK
    xt = jnp.transpose(spectrum, (2, 0, 1))
    maskf = ocean_mask.astype(jnp.float32)
    current = jnp.broadcast_to(u_current[:, None], (rows, LANES))
    angles = (2.0 * math.pi * np.arange(ndirs, dtype=np.float32) / ndirs).astype(np.float32)
    cosines = jnp.asarray(np.cos(angles.astype(np.float64)).astype(np.float32))
    sines = jnp.asarray(np.sin(angles.astype(np.float64)).astype(np.float32))
    vmem = pl.BlockSpec(memory_space=pltpu.VMEM)
    smem = pl.BlockSpec(memory_space=pltpu.SMEM)
    dma = pltpu.SemaphoreType.DMA
    tile = (ROWS, LANES)

    def scratch(*lead):
        return pltpu.VMEM(lead + tile, jnp.float32)

    return pl.pallas_call(
        functools.partial(kernel, (ncomp, nspace, ndirs, nfreqs, per_core)),
        out_shape=jax.ShapeDtypeStruct((owned, ndirs, rows, LANES), jnp.float32),
        in_specs=[vmem] * 6 + [smem] * 6,
        out_specs=pl.BlockSpec(memory_space=pl.ANY),
        scratch_shapes=[
            scratch(nd),
            pltpu.VMEM((4, ROWS, strip), jnp.float32),
            scratch(npeer, per_core, nd),
            scratch(npeer, per_core, nd),
            scratch(per_core, 2, ndirs),
            scratch(3),
            scratch(3),
            scratch(2),
            scratch(2),
            scratch(6),
            scratch(2, 5),
            scratch(2, per_core, 2 * packs),
            scratch(2, per_core, 2 * packs),
            scratch(2, 2, ndirs),
            scratch(per_core, 2, ndirs),
            dma((npeer, per_core)),
            dma((npeer, per_core)),
            dma((5,)),
            dma((5,)),
            dma((2, per_core)),
            dma((2, per_core)),
            dma((per_core,)),
            dma((per_core,)),
            dma((per_core,)),
        ],
        compiler_params=pltpu.CompilerParams(
            collective_id=0, has_side_effects=True, vmem_limit_bytes=40 * 1024 * 1024
        ),
        cost_estimate=pl.CostEstimate(flops=80_000_000, bytes_accessed=8_000_000, transcendentals=442368),
    )(
        xt,
        wind_speed,
        wind_dir,
        maskf,
        turning,
        current,
        group_courant,
        growth_rate,
        dissipation,
        comp_owner,
        cosines,
        sines,
    )


def solution(mesh):
    placed = (
        P(("groups", "sub"), ("space", "comp"), None),
        P(("groups", "sub"), ("space", "comp")),
        P(("groups", "sub"), ("space", "comp")),
        P("sub", "space"),
        P("sub", "space"),
        P("sub"),
        P(),
        P(),
        P(),
        P(),
    )
    return jax.shard_map(
        functools.partial(per_device, mesh.shape["comp"], mesh.shape["space"]),
        mesh=mesh,
        in_specs=placed,
        out_specs=P("comp", None, ("groups", "sub"), "space"),
        check_vma=False,
    )
```

profile of v0, /device:TPU:0, one launch (start us, length us, event | category | flops | bytes accessed | tf_op | source)
XLA Modules:
  0.0 168.0 jit_solution(8492362417015910968)
XLA Ops:
  0.0 0.7 convert_element_type.3.mask
  0.7 0.7 broadcast_in_dim.2.current
  1.4 0.0 copy-start
  1.4 0.0 copy-start.1
  1.4 3.0 %copy.13 = f32[8,64,864]{1,0,2:T(8,128)S(1)} copy(f32[8,64,864]{2,1,0:T(8,128)} %param.12) | data formatting | bytes 3538944 | tf_op args[0]
  4.4 0.0 copy-done
  4.4 0.0 copy-done.1
  4.4 0.0 copy-start.2
  4.4 0.7 copy-done.2
  5.1 0.0 copy-start.3
  5.1 0.7 copy-done.3
  5.7 0.0 copy-start.4
  5.7 0.7 copy-done.4
  6.4 0.0 copy-start.5
  6.4 0.7 copy-done.5
  7.1 0.0 copy-start.6
  7.1 0.7 copy-done.6
  7.7 0.0 copy-start.7
  7.7 0.7 copy-done.7
  8.4 0.0 copy-start.8
  8.4 0.7 copy-done.8
  9.0 157.7 %shard_map.118 = f32[12,36,8,128]{3,2,1,0:T(8,128)S(1)} custom-call(f32[864,8,64]{2,1,0:T(8,128)S(1)} %bitcast.1, f32[8,64]{1,0:T(8,128)S(1)} %copy-done, f32[8,64]{1,0:T(8,128)S(1)} %copy-done.1, f32[8,128]{1,0:T(8,128)S(1)} %convert_element_type.3.mask, f32[8,128]{1,0:T(8,128)S(1)} %copy-done.2, f32[8,128]{1,0:T(8,128)S(1)} %broadcast_in_dim.2.current, ...), custom_call_target="tpu_custom_call" | custom-call | flops 80000000 | bytes 8000000 | tf_op jit(solution)/shard_map/pallas_call | solution.py:430
  166.7 1.2 copy.15
Async XLA Ops:
  1.4 3.0 %copy-start = (f32[8,64]{1,0:T(8,128)S(1)}, f32[8,64]{1,0:T(8,128)}, u32[]{:S(2)}) copy-start(f32[8,64]{1,0:T(8,128)} %wind_speed.1) | copy-start | bytes 6148
  1.4 3.0 %copy-start.1 = (f32[8,64]{1,0:T(8,128)S(1)}, f32[8,64]{1,0:T(8,128)}, u32[]{:S(2)}) copy-start(f32[8,64]{1,0:T(8,128)} %wind_dir.1) | copy-start | bytes 6148
  4.4 0.7 copy-start.2
  5.1 0.7 copy-start.3
  5.7 0.7 copy-start.4
  6.4 0.7 copy-start.5
  7.1 0.7 copy-start.6
  7.7 0.7 copy-start.7
  8.4 0.7 copy-start.8
where the time goes:
time: 168 us
  Pallas kernels  158 us (94%)
  local copies, waits for them, and re-layouts  9.51 us (6%)
    pallas_call x1, Pallas kernels, per_device(): pl.pallas_call(functools.partial(kernel, (ncomp, nspace, ndirs, nfreqs, p...  158 us
    unnamed x20, local copies, waits for them, and re-layouts  8.78 us

commit v1 on v0

--- a/solution.py
+++ b/solution.py
@@ -34,14 +34,18 @@
     wind_dir,
     mask,
     turning,
+    current_hbm,
+    speed_hbm,
+    growth_hbm,
+    loss_hbm,
+    owner_hbm,
+    out,
     current,
     speed,
     growth,
     loss,
     owner,
-    cosines,
-    sines,
-    out,
+    param_sem,
     tables,
     level_part,
     sendbuf,
@@ -55,6 +59,7 @@
     turn_all,
     halo_out,
     halo_in,
+    lon_w,
     spin,
     res,
     send_sem,
@@ -79,6 +84,9 @@
     right = lax.rem(me_z + 1, nspace)
     left = lax.rem(me_z + nspace - 1, nspace)
     MESH = pl.DeviceIdType.MESH
+    angles = (2.0 * math.pi * np.arange(ndirs, dtype=np.float32) / ndirs).astype(np.float64)
+    cosines = [float(np.float32(np.cos(a))) for a in angles]
+    sines = [float(np.float32(np.sin(a))) for a in angles]
     lane = lax.broadcasted_iota(jnp.int32, (ROWS, LANES), 1)
     row = lax.broadcasted_iota(jnp.int32, (ROWS, LANES), 0)
 
@@ -93,6 +101,18 @@
     for to in near:
         pl.semaphore_signal(barrier, inc=1, device_id=to, device_id_type=MESH)
 
+    params = [
+        pltpu.make_async_copy(src, dst, param_sem.at[i])
+        for i, (src, dst) in enumerate((
+            (current_hbm, current),
+            (speed_hbm, speed),
+            (growth_hbm, growth),
+            (loss_hbm, loss),
+            (owner_hbm, owner),
+        ))
+    ]
+    for copy in params:
+        copy.start()
     level_part[...] = jnp.zeros_like(level_part)
 
     def add_level(f, carry):
@@ -116,9 +136,14 @@
         angle = 2.0 * math.pi * (group + dd).astype(jnp.float32) / ndirs
         tables[dd] = wind * jnp.maximum(jnp.cos(angle - toward), 0.0)
 
-    small[0] = mask[...]
+    for copy in params:
+        copy.wait()
+    flow = jnp.zeros((ROWS, LANES), jnp.float32)
+    for j in range(ROWS):
+        flow = jnp.where(row == j, current[j], flow)
+    small[0] = mask[...].astype(jnp.float32)
     small[1] = turning[...]
-    small[2] = current[...]
+    small[2] = flow
     pl.semaphore_wait(barrier, len(peers) + len(near))
 
     def fill(dst, at, co, so, kk):
@@ -243,27 +268,18 @@
                         tile = jnp.where(lane < c * strip, tile, part)
                     main[kk, h, g * nd + dd] = tile * sea
             for q in range(packs):
-                lows = jnp.zeros((ROWS, LANES), jnp.float32)
-                highs = lows
+                lows = highs = None
                 for j in range(PER_PACK):
                     tile = main[kk, h, q * PER_PACK + j]
                     at = j * HALO
-                    here = (lane >= at) & (lane < at + HALO)
                     low = tile if at == 0 else pltpu.roll(tile, at, 1)
-                    lows = jnp.where(here, low, lows)
-                    highs = jnp.where(here, pltpu.roll(tile, at + HALO, 1), highs)
+                    high = pltpu.roll(tile, at + HALO, 1)
+                    lows = low if j == 0 else jnp.where(lane < at, lows, low)
+                    highs = high if j == 0 else jnp.where(lane < at, highs, high)
                 halo_out[0, kk, h * packs + q] = lows
                 halo_out[1, kk, h * packs + q] = highs
         halo_copy(0, kk).start()
         halo_copy(1, kk).start()
-
-    def along_lon(f, w, up, sea):
-        up2, before, mid, after = w
-        for _ in range(NSUB):
-            far = jnp.where(up, pltpu.roll(f, 2, 1), pltpu.roll(f, LANES - 2, 1))
-            near_sum = before * pltpu.roll(f, 1, 1) + after * pltpu.roll(f, LANES - 1, 1)
-            f = (mid * f + up2 * far + near_sum) * sea
-        return f
 
     def along_lat(lo, hi, c, forward, sea_lo, sea_hi):
         up2, up1, mid, down = weights(c)
@@ -300,45 +316,58 @@
         k = (me_c * 2 + me_s) * per_core + kk
         pace = speed[owner[k]]
 
-        def one(q, j, d, forward):
-            lo, hi = main[kk, 0, d], main[kk, 1, d]
-            edge = jnp.zeros((ROWS, LANES), jnp.float32)
-            for h, tile in ((0, lo), (1, hi)):
-                base = 64 * h
-                before = halo_in[1, kk, h * packs + q]
-                after = halo_in[0, kk, h * packs + q]
-                for source, start, count, at in (
-                    (tile, LANES - 16, 16, 0),
-                    (after, j * HALO, HALO, 16),
-                    (before, j * HALO, HALO, 24),
-                    (tile, 0, 16, 32),
-                ):
-                    amount = (base + at - start) % LANES
-                    moved = source if amount == 0 else pltpu.roll(source, amount, 1)
-                    here = (lane >= base + at) & (lane < base + at + count)
-                    edge = jnp.where(here, moved, edge)
-            c0 = pace * cosines[d]
-            done = []
-            for i, tile in enumerate((lo, hi, edge)):
-                c = c0 + mask_all[3 + i]
-                up2, up1, mid, down = weights(c)
-                up = c > 0
-                w = (up2, jnp.where(up, up1, down), mid, jnp.where(up, down, up1))
-                done.append(along_lon(tile, w, up, mask_all[i]))
-            lo, hi, edge = done
-            fixed = []
-            for h, tile in ((0, lo), (1, hi)):
-                base = 64 * h
-                tile = jnp.where(lane < HALO, pltpu.roll(edge, (LANES - base - 32) % LANES, 1), tile)
-                tile = jnp.where(
-                    lane >= LANES - HALO, pltpu.roll(edge, (LANES - 16 - base) % LANES, 1), tile)
-                fixed.append(tile)
-            lo, hi = along_lat(fixed[0], fixed[1], pace * sines[d], forward, mask_all[0], mask_all[1])
-            spin[0, 0, d] = lo
-            spin[0, 1, d] = hi
-
-        for d in range(ndirs):
-            one(d // PER_PACK, d % PER_PACK, d, d < half)
+        for q in range(packs):
+            fields = []
+            for j in range(PER_PACK):
+                d = q * PER_PACK + j
+                pieces = []
+                for h in range(2):
+                    tile = main[kk, h, d]
+                    for source, start, at, end in (
+                        (tile, LANES - 16, 0, 16),
+                        (halo_in[0, kk, h * packs + q], j * HALO, 16, 24),
+                        (halo_in[1, kk, h * packs + q], j * HALO, 24, 32),
+                        (tile, 0, 32, 64),
+                    ):
+                        amount = (64 * h + at - start) % LANES
+                        moved = source if amount == 0 else pltpu.roll(source, amount, 1)
+                        pieces.append((64 * h + end, moved))
+                edge = pieces[-1][1]
+                for end, moved in reversed(pieces[:-1]):
+                    edge = jnp.where(lane < end, moved, edge)
+                c0 = pace * cosines[d]
+                for i, tile in enumerate((main[kk, 0, d], main[kk, 1, d], edge)):
+                    c = c0 + mask_all[3 + i]
+                    up2, up1, mid, down = weights(c)
+                    up = c > 0
+                    lon_w[j * 3 + i, 0] = up2
+                    lon_w[j * 3 + i, 1] = jnp.where(up, up1, down)
+                    lon_w[j * 3 + i, 2] = mid
+                    lon_w[j * 3 + i, 3] = jnp.where(up, down, up1)
+                    lon_w[j * 3 + i, 4] = c
+                    fields.append(tile)
+            for step in range(NSUB):
+                for n, f in enumerate(fields):
+                    far = jnp.where(
+                        lon_w[n, 4] > 0, pltpu.roll(f, 2, 1), pltpu.roll(f, LANES - 2, 1))
+                    near_sum = lon_w[n, 1] * pltpu.roll(f, 1, 1) + lon_w[n, 3] * pltpu.roll(f, LANES - 1, 1)
+                    f = (lon_w[n, 2] * f + lon_w[n, 0] * far + near_sum) * mask_all[n % 3]
+                    fields[n] = f
+            for j in range(PER_PACK):
+                d = q * PER_PACK + j
+                edge = fields[3 * j + 2]
+                fixed = []
+                for h in range(2):
+                    base = 64 * h
+                    tile = fields[3 * j + h]
+                    head = pltpu.roll(edge, (LANES - base - 32) % LANES, 1)
+                    tail = pltpu.roll(edge, (LANES - 16 - base) % LANES, 1)
+                    tile = jnp.where(lane < HALO, head, tile)
+                    fixed.append(jnp.where(lane < LANES - HALO, tile, tail))
+                lo, hi = along_lat(
+                    fixed[0], fixed[1], pace * sines[d], d < half, mask_all[0], mask_all[1])
+                spin[0, 0, d] = lo
+                spin[0, 1, d] = hi
 
         def turn(h, carry):
             up2, up1, mid, down = (turn_all[h, i] for i in range(4))
@@ -414,13 +443,7 @@
     npeer = ncomp * 2
     packs = ndirs // PER_PACK
     xt = jnp.transpose(spectrum, (2, 0, 1))
-    maskf = ocean_mask.astype(jnp.float32)
-    current = jnp.broadcast_to(u_current[:, None], (rows, LANES))
-    angles = (2.0 * math.pi * np.arange(ndirs, dtype=np.float32) / ndirs).astype(np.float32)
-    cosines = jnp.asarray(np.cos(angles.astype(np.float64)).astype(np.float32))
-    sines = jnp.asarray(np.sin(angles.astype(np.float64)).astype(np.float32))
     vmem = pl.BlockSpec(memory_space=pltpu.VMEM)
-    smem = pl.BlockSpec(memory_space=pltpu.SMEM)
     dma = pltpu.SemaphoreType.DMA
     tile = (ROWS, LANES)
 
@@ -430,9 +453,15 @@
     return pl.pallas_call(
         functools.partial(kernel, (ncomp, nspace, ndirs, nfreqs, per_core)),
         out_shape=jax.ShapeDtypeStruct((owned, ndirs, rows, LANES), jnp.float32),
-        in_specs=[vmem] * 6 + [smem] * 6,
+        in_specs=[vmem] * 5 + [pl.BlockSpec(memory_space=pl.ANY)] * 5,
         out_specs=pl.BlockSpec(memory_space=pl.ANY),
         scratch_shapes=[
+            pltpu.SMEM((rows,), jnp.float32),
+            pltpu.SMEM((nfreqs,), jnp.float32),
+            pltpu.SMEM((nfreqs,), jnp.float32),
+            pltpu.SMEM((nfreqs,), jnp.float32),
+            pltpu.SMEM((nfreqs,), jnp.int32),
+            dma((5,)),
             scratch(nd),
             pltpu.VMEM((4, ROWS, strip), jnp.float32),
             scratch(npeer, per_core, nd),
@@ -446,6 +475,7 @@
             scratch(2, 5),
             scratch(2, per_core, 2 * packs),
             scratch(2, per_core, 2 * packs),
+            scratch(3 * PER_PACK, 5),
             scratch(2, 2, ndirs),
             scratch(per_core, 2, ndirs),
             dma((npeer, per_core)),
@@ -466,15 +496,13 @@
         xt,
         wind_speed,
         wind_dir,
-        maskf,
+        ocean_mask,
         turning,
-        current,
+        u_current,
         group_courant,
         growth_rate,
         dissipation,
         comp_owner,
-        cosines,
-        sines,
     )
 
 

time: 168 us -> 46.3 us (0.28)
  Pallas kernels: 158 us -> 38.6 us
  local copies, waits for them, and re-layouts: 9.51 us -> 7.48 us
    pallas_call x1, Pallas kernels: 158 us -> 38.6 us  [per_device(): pl.pallas_call(functools.partial(kernel, (ncomp, nspace, ndirs, nfreqs, p...]
where the time goes in v1:
time: 46.3 us; the launch traced here: 46.1 us
  Pallas kernels  38.6 us (83%)
  local copies, waits for them, and re-layouts  7.48 us (16%)
    pallas_call x1, Pallas kernels, per_device(): pl.pallas_call(functools.partial(kernel, (ncomp, nspace, ndirs, nfreqs, p...  38.6 us
    unnamed x20, local copies, waits for them, and re-layouts  7.48 us

profile of v1, /device:TPU:0, one launch (start us, length us, event | category | flops | bytes accessed | tf_op | source)
XLA Modules:
  0.0 46.1 jit_solution(1301891081166074720)
XLA Ops:
  0.0 0.0 copy-start.3
  0.0 0.0 copy-start.2
  0.0 0.0 copy-start.1
  0.0 0.0 copy-start
  0.0 3.0 %copy.11 = f32[8,64,864]{1,0,2:T(8,128)S(1)} copy(f32[8,64,864]{2,1,0:T(8,128)} %param.10) | data formatting | bytes 3538944 | tf_op args[0]
  3.0 0.0 copy-done.3
  3.0 0.0 copy-done.2
  3.0 0.0 copy-done.1
  3.0 0.0 copy-done
  3.0 0.0 copy-start.4
  3.1 0.6 %copy-done.4 = f32[8]{0:T(128)S(1)} copy-done((f32[8]{0:T(128)S(1)}, f32[8]{0:T(128)}, u32[]{:S(2)}) %copy-start.4) | copy-done | bytes 56
  3.7 0.0 copy-start.5
  3.7 0.7 %copy-done.5 = f32[24]{0:T(128)S(1)} copy-done((f32[24]{0:T(128)S(1)}, f32[24]{0:T(128)}, u32[]{:S(2)}) %copy-start.5) | copy-done | bytes 120
  4.4 0.0 copy-start.6
  4.4 0.7 %copy-done.6 = f32[24]{0:T(128)S(1)} copy-done((f32[24]{0:T(128)S(1)}, f32[24]{0:T(128)}, u32[]{:S(2)}) %copy-start.6) | copy-done | bytes 120
  5.0 0.0 copy-start.7
  5.0 0.7 %copy-done.7 = f32[24]{0:T(128)S(1)} copy-done((f32[24]{0:T(128)S(1)}, f32[24]{0:T(128)}, u32[]{:S(2)}) %copy-start.7) | copy-done | bytes 120
  5.7 0.0 copy-start.8
  5.7 0.7 %copy-done.8 = s32[24]{0:T(128)S(1)} copy-done((s32[24]{0:T(128)S(1)}, s32[24]{0:T(128)}, u32[]{:S(2)}) %copy-start.8) | copy-done | bytes 120
  6.3 38.6 %shard_map.100 = f32[12,36,8,128]{3,2,1,0:T(8,128)S(1)} custom-call(f32[864,8,64]{2,1,0:T(8,128)S(1)} %bitcast.1, f32[8,64]{1,0:T(8,128)S(1)} %copy-done, f32[8,64]{1,0:T(8,128)S(1)} %copy-done.1, s32[8,128]{1,0:T(8,128)S(1)} %copy-done.2, f32[8,128]{1,0:T(8,128)S(1)} %copy-done.3, f32[8]{0:T(128)S(1)} %copy-done.4, f32[24]{0:T(128)S(1)} %copy-done.5, ...), custom_call_target="tpu_custom_call" | custom-call | flops 80000000 | bytes 8000000 | tf_op jit(solution)/shard_map/pallas_call | solution.py:453
  44.9 1.2 %copy.13 = f32[12,36,8,128]{3,2,1,0:T(8,128)} copy(f32[12,36,8,128]{3,2,1,0:T(8,128)S(1)} %shard_map.100) | data formatting | bytes 3538944
Async XLA Ops:
  0.0 3.0 %copy-start.3 = (f32[8,128]{1,0:T(8,128)S(1)}, f32[8,128]{1,0:T(8,128)}, u32[]{:S(2)}) copy-start(f32[8,128]{1,0:T(8,128)} %turning.1) | copy-start | bytes 12292
  0.0 3.0 %copy-start.2 = (s32[8,128]{1,0:T(8,128)S(1)}, s32[8,128]{1,0:T(8,128)}, u32[]{:S(2)}) copy-start(s32[8,128]{1,0:T(8,128)} %mask.1) | copy-start | bytes 12292
  0.0 3.0 %copy-start.1 = (f32[8,64]{1,0:T(8,128)S(1)}, f32[8,64]{1,0:T(8,128)}, u32[]{:S(2)}) copy-start(f32[8,64]{1,0:T(8,128)} %wind_dir.1) | copy-start | bytes 6148
  0.0 3.0 %copy-start = (f32[8,64]{1,0:T(8,128)S(1)}, f32[8,64]{1,0:T(8,128)}, u32[]{:S(2)}) copy-start(f32[8,64]{1,0:T(8,128)} %wind_speed.1) | copy-start | bytes 6148
  3.0 0.7 %copy-start.4 = (f32[8]{0:T(128)S(1)}, f32[8]{0:T(128)}, u32[]{:S(2)}) copy-start(f32[8]{0:T(128)} %current_hbm.1) | copy-start | bytes 100
  3.7 0.7 %copy-start.5 = (f32[24]{0:T(128)S(1)}, f32[24]{0:T(128)}, u32[]{:S(2)}) copy-start(f32[24]{0:T(128)} %speed_hbm.1) | copy-start | bytes 292
  4.4 0.7 %copy-start.6 = (f32[24]{0:T(128)S(1)}, f32[24]{0:T(128)}, u32[]{:S(2)}) copy-start(f32[24]{0:T(128)} %growth_hbm.1) | copy-start | bytes 292
  5.0 0.7 %copy-start.7 = (f32[24]{0:T(128)S(1)}, f32[24]{0:T(128)}, u32[]{:S(2)}) copy-start(f32[24]{0:T(128)} %loss_hbm.1) | copy-start | bytes 292
  5.7 0.7 %copy-start.8 = (s32[24]{0:T(128)S(1)}, s32[24]{0:T(128)}, u32[]{:S(2)}) copy-start(s32[24]{0:T(128)} %owner_hbm.1) | copy-start | bytes 292

commit v2 on v1

--- a/solution.py
+++ b/solution.py
@@ -34,16 +34,10 @@
     wind_dir,
     mask,
     turning,
-    current_hbm,
-    speed_hbm,
-    growth_hbm,
-    loss_hbm,
+    rates_hbm,
     owner_hbm,
     out,
-    current,
-    speed,
-    growth,
-    loss,
+    rates,
     owner,
     param_sem,
     tables,
@@ -104,10 +98,7 @@
     params = [
         pltpu.make_async_copy(src, dst, param_sem.at[i])
         for i, (src, dst) in enumerate((
-            (current_hbm, current),
-            (speed_hbm, speed),
-            (growth_hbm, growth),
-            (loss_hbm, loss),
+            (rates_hbm, rates),
             (owner_hbm, owner),
         ))
     ]
@@ -140,7 +131,7 @@
         copy.wait()
     flow = jnp.zeros((ROWS, LANES), jnp.float32)
     for j in range(ROWS):
-        flow = jnp.where(row == j, current[j], flow)
+        flow = jnp.where(row == j, rates[3 * nfreqs + j], flow)
     small[0] = mask[...].astype(jnp.float32)
     small[1] = turning[...]
     small[2] = flow
@@ -150,8 +141,8 @@
         dest = peer(co, so)
         k = (dest["comp"] * 2 + dest["sub"]) * per_core + kk
         f = owner[k]
-        g_rate = growth[f]
-        d_rate = loss[f]
+        g_rate = rates[nfreqs + f]
+        d_rate = rates[2 * nfreqs + f]
         for dd in range(nd):
             parts = [xt[f * ndirs + g * nd + dd] for g in range(ncomp)]
             tile = jnp.concatenate(parts, axis=1)
@@ -314,7 +305,7 @@
         halo_copy(0, kk).wait_recv()
         halo_copy(1, kk).wait_recv()
         k = (me_c * 2 + me_s) * per_core + kk
-        pace = speed[owner[k]]
+        pace = rates[owner[k]]
 
         for q in range(packs):
             fields = []
@@ -443,6 +434,7 @@
     npeer = ncomp * 2
     packs = ndirs // PER_PACK
     xt = jnp.transpose(spectrum, (2, 0, 1))
+    rates = jnp.concatenate([group_courant, growth_rate, dissipation, u_current])
     vmem = pl.BlockSpec(memory_space=pltpu.VMEM)
     dma = pltpu.SemaphoreType.DMA
     tile = (ROWS, LANES)
@@ -453,15 +445,12 @@
     return pl.pallas_call(
         functools.partial(kernel, (ncomp, nspace, ndirs, nfreqs, per_core)),
         out_shape=jax.ShapeDtypeStruct((owned, ndirs, rows, LANES), jnp.float32),
-        in_specs=[vmem] * 5 + [pl.BlockSpec(memory_space=pl.ANY)] * 5,
+        in_specs=[vmem] * 5 + [pl.BlockSpec(memory_space=pl.ANY)] * 2,
         out_specs=pl.BlockSpec(memory_space=pl.ANY),
         scratch_shapes=[
-            pltpu.SMEM((rows,), jnp.float32),
-            pltpu.SMEM((nfreqs,), jnp.float32),
-            pltpu.SMEM((nfreqs,), jnp.float32),
-            pltpu.SMEM((nfreqs,), jnp.float32),
+            pltpu.SMEM((3 * nfreqs + rows,), jnp.float32),
             pltpu.SMEM((nfreqs,), jnp.int32),
-            dma((5,)),
+            dma((2,)),
             scratch(nd),
             pltpu.VMEM((4, ROWS, strip), jnp.float32),
             scratch(npeer, per_core, nd),
@@ -498,10 +487,7 @@
         wind_dir,
         ocean_mask,
         turning,
-        u_current,
-        group_courant,
-        growth_rate,
-        dissipation,
+        rates,
         comp_owner,
     )
 

time: 46.3 us -> 45.3 us (0.978)
  local copies, waits for them, and re-layouts: 7.48 us -> 5.51 us
  other arithmetic: 0 us -> 1.29 us
    unnamed x20 -> x14, local copies, waits for them, and re-layouts: 7.48 us -> 5.51 us
    concatenate x0 -> x1, other arithmetic: none -> 1.29 us  [per_device(): jnp.concatenate([group_courant, growth_rate, dissipation, u_current])]
where the time goes in v2:
time: 45.3 us; the launch traced here: 45.2 us
  Pallas kernels  38.3 us (85%)
  local copies, waits for them, and re-layouts  5.51 us (12%)
  other arithmetic  1.29 us (3%)
    pallas_call x1, Pallas kernels, per_device(): pl.pallas_call(functools.partial(kernel, (ncomp, nspace, ndirs, nfreqs, p...  38.3 us
    unnamed x14, local copies, waits for them, and re-layouts  5.51 us
    concatenate x1, other arithmetic, per_device(): jnp.concatenate([group_courant, growth_rate, dissipation, u_current])  1.29 us

profile of v2, /device:TPU:0, one launch (start us, length us, event | category | flops | bytes accessed | tf_op | source)
XLA Modules:
  0.0 45.2 jit_solution(15512534175056192114)
XLA Ops:
  0.0 1.3 %pad_maximum_fusion.rates_hbm = f32[80]{0:T(128)} fusion(f32[8]{0:T(128)} %param.15, f32[24]{0:T(128)} %param.18, f32[24]{0:T(128)} %param.17, f32[24]{0:T(128)} %param.16), kind=kLoop, calls=%fused_computation | loop fusion | flops 240 | bytes 640 | tf_op jit(solution)/shard_map/concatenate | solution.py:437
  1.3 0.0 copy-start
  1.3 0.0 copy-start.1
  1.3 0.0 copy-start.2
  1.3 0.0 copy-start.3
  1.3 3.0 %copy.11 = f32[8,64,864]{1,0,2:T(8,128)S(1)} copy(f32[8,64,864]{2,1,0:T(8,128)} %param.10) | data formatting | bytes 3538944 | tf_op args[0]
  4.3 0.0 copy-done
  4.3 0.0 copy-done.1
  4.3 0.0 copy-done.2
  4.3 0.0 copy-done.3
  4.3 0.0 copy-start.4
  4.3 0.6 %copy-done.4 = f32[80]{0:T(128)S(1)} copy-done((f32[80]{0:T(128)S(1)}, f32[80]{0:T(128)}, u32[]{:S(2)}) %copy-start.4) | copy-done | bytes 344
  5.0 0.0 copy-start.5
  5.0 0.7 %copy-done.5 = s32[24]{0:T(128)S(1)} copy-done((s32[24]{0:T(128)S(1)}, s32[24]{0:T(128)}, u32[]{:S(2)}) %copy-start.5) | copy-done | bytes 120
  5.6 38.3 %shard_map.100 = f32[12,36,8,128]{3,2,1,0:T(8,128)S(1)} custom-call(f32[864,8,64]{2,1,0:T(8,128)S(1)} %bitcast.1, f32[8,64]{1,0:T(8,128)S(1)} %copy-done, f32[8,64]{1,0:T(8,128)S(1)} %copy-done.1, s32[8,128]{1,0:T(8,128)S(1)} %copy-done.2, f32[8,128]{1,0:T(8,128)S(1)} %copy-done.3, f32[80]{0:T(128)S(1)} %copy-done.4, s32[24]{0:T(128)S(1)} %copy-done.5), custom_call_target="tpu_custom_call" | custom-call | flops 80000000 | bytes 8000000 | tf_op jit(solution)/shard_map/pallas_call | solution.py:445
  43.9 1.2 %copy.13 = f32[12,36,8,128]{3,2,1,0:T(8,128)} copy(f32[12,36,8,128]{3,2,1,0:T(8,128)S(1)} %shard_map.100) | data formatting | bytes 3538944
Async XLA Ops:
  1.3 3.0 %copy-start = (f32[8,64]{1,0:T(8,128)S(1)}, f32[8,64]{1,0:T(8,128)}, u32[]{:S(2)}) copy-start(f32[8,64]{1,0:T(8,128)} %wind_speed.1) | copy-start | bytes 6148
  1.3 3.0 %copy-start.1 = (f32[8,64]{1,0:T(8,128)S(1)}, f32[8,64]{1,0:T(8,128)}, u32[]{:S(2)}) copy-start(f32[8,64]{1,0:T(8,128)} %wind_dir.1) | copy-start | bytes 6148
  1.3 3.0 %copy-start.2 = (s32[8,128]{1,0:T(8,128)S(1)}, s32[8,128]{1,0:T(8,128)}, u32[]{:S(2)}) copy-start(s32[8,128]{1,0:T(8,128)} %mask.1) | copy-start | bytes 12292
  1.3 3.0 %copy-start.3 = (f32[8,128]{1,0:T(8,128)S(1)}, f32[8,128]{1,0:T(8,128)}, u32[]{:S(2)}) copy-start(f32[8,128]{1,0:T(8,128)} %turning.1) | copy-start | bytes 12292
  4.3 0.7 %copy-start.4 = (f32[80]{0:T(128)S(1)}, f32[80]{0:T(128)}, u32[]{:S(2)}) copy-start(f32[80]{0:T(128)} %pad_maximum_fusion.rates_hbm) | copy-start | bytes 964
  5.0 0.7 %copy-start.5 = (s32[24]{0:T(128)S(1)}, s32[24]{0:T(128)}, u32[]{:S(2)}) copy-start(s32[24]{0:T(128)} %owner_hbm.1) | copy-start | bytes 292
